TPU v7x, 128 devices: a whole 4x4x4 slice. The times are simulated.
128 devices in a mesh: ctx: 16 (over y_hi, z, core), tp: 8 (over y_lo, x).
Axes of the slice: x: 4, y: 4 (y_hi: 2, y_lo: 2; y = y_hi * 2 + y_lo), z: 4, core: 2. Of those that a mesh axis runs over, the one named last changes fastest.
Arguments:
- grad_out: bfloat16 [10240, 4096], P(('ctx', 'tp')), may hold values from -3 to 3
- expert_ids: int32 [10240, 8], P(('ctx', 'tp')), may hold values from 0 to 63, all different within a row; in each aligned block of 80 rows (0 to 79, 80 to 159, ...) at most 12 rows name the same one
- combine: bfloat16 [10240, 8], P(('ctx', 'tp')), may hold values from 0.049804688 to 0.5
- gate_saved: bfloat16 [128, 12, 98304], P(None, None, ('ctx', 'tp')), may hold values from -5 to 5
- up_saved: bfloat16 [128, 12, 98304], P(None, None, ('ctx', 'tp')), may hold values from -5 to 5
- gate_weight: bfloat16 [4096, 98304], P(None, ('ctx', 'tp')), may hold values from -0.09375 to 0.09375
- up_weight: bfloat16 [4096, 98304], P(None, ('ctx', 'tp')), may hold values from -0.09375 to 0.09375
- down_weight: bfloat16 [98304, 4096], P(('ctx', 'tp')), may hold values from -0.15625 to 0.15625
Outputs:
- grad_in: bfloat16 [10240, 4096], P(('ctx', 'tp'))
- grad_combine: bfloat16 [10240, 8], P(('ctx', 'tp'))
Inputs may be any that keep to these rules, and one draw needn't show every extreme that they name: `expert_ids`: each row names 8 different experts. The rows of one device name any one expert at most 12 times, a bound that some block reaches.
All inputs are finite; a program needn't handle non-finite values.
Results may differ from a plain program's by a relative error of at most 0.0065.
Values may be sent and summed in bfloat16 or wider, within the bound.
A program may use at most 192 MiB of HBM per device.

v0:
```python
import jax
import jax.numpy as jnp
from jax import lax
from jax.sharding import PartitionSpec as P


def swapped(value, axis, stride):
    return lax.ppermute(value, axis, [(i, i ^ 1 << stride) for i in range(lax.axis_size(axis))])


def body(grad_out, expert_ids, combine, gate_saved, up_saved, gate_weight, up_weight, down_weight):
    tok_count = grad_out.shape[0]
    top_count = expert_ids.shape[1]
    width = grad_out.shape[1]
    half_cols = width // 2
    sources = gate_saved.shape[0]
    capacity = gate_saved.shape[1]
    half_width = gate_weight.shape[1]
    experts = sources // 2
    flat_ids = expert_ids.reshape(-1)
    one_hot = (flat_ids[:, None] == jnp.arange(experts, dtype=jnp.int32)[None, :]).astype(jnp.int32)
    before = jnp.cumsum(one_hot, axis=0) - one_hot
    position = jnp.sum(before * one_hot, axis=1)
    slot_id = flat_ids * capacity + position
    chosen = (slot_id[:, None] == jnp.arange(experts * capacity, dtype=jnp.int32)[None, :]).astype(
        jnp.float32
    )
    placing = jnp.sum(chosen.reshape(tok_count, top_count, experts * capacity), axis=1).astype(
        jnp.bfloat16
    )
    outbound = jnp.dot(placing.T, grad_out, preferred_element_type=jnp.float32).astype(jnp.bfloat16)
    slot_weight = jnp.dot(
        combine.reshape(1, -1).astype(jnp.float32), chosen, precision=lax.Precision.HIGHEST
    )[0].astype(jnp.bfloat16)
    parity = lax.axis_index("tp") % 2
    send_rows = jnp.broadcast_to(
        outbound.reshape(experts, 1, capacity, width), (experts, 2, capacity, width)
    ).reshape(sources, capacity, width)
    send_weights = jnp.broadcast_to(
        slot_weight.reshape(experts, 1, capacity), (experts, 2, capacity)
    ).reshape(sources, capacity)
    arrived, arrived_w = (
        lax.all_to_all(send_rows, ("ctx", "tp"), split_axis=0, concat_axis=0, tiled=True),
        lax.all_to_all(send_weights, ("ctx", "tp"), split_axis=0, concat_axis=0, tiled=True),
    )
    row_count = sources * capacity
    grad_rows = arrived.reshape(row_count, width)
    gate_pre = gate_saved.reshape(row_count, half_width).astype(jnp.float32)
    up_vals = up_saved.reshape(row_count, half_width).astype(jnp.float32)
    hidden_grad = lax.dot_general(
        grad_rows, down_weight, (((1,), (1,)), ((), ())), preferred_element_type=jnp.float32
    )
    sigmoid_g = jax.nn.sigmoid(gate_pre)
    activated = gate_pre * sigmoid_g
    comb_part = jnp.sum(activated * up_vals * hidden_grad, axis=1).astype(jnp.bfloat16)
    weighted = hidden_grad * arrived_w.reshape(row_count, 1).astype(jnp.float32)
    dgate = (weighted * up_vals * sigmoid_g * (1.0 + gate_pre * (1.0 - sigmoid_g))).astype(
        jnp.bfloat16
    )
    dup = (weighted * activated).astype(jnp.bfloat16)
    partial_value = lax.dot_general(
        dgate, gate_weight, (((1,), (1,)), ((), ())), preferred_element_type=jnp.float32
    )
    partial_value = partial_value + lax.dot_general(
        dup, up_weight, (((1,), (1,)), ((), ())), preferred_element_type=jnp.float32
    )
    partial_value = partial_value.astype(jnp.bfloat16).reshape(sources, capacity, width)
    comb_part = comb_part.reshape(sources, capacity)
    kept_rows = jnp.where(
        parity == 0, partial_value[:, :, :half_cols], partial_value[:, :, half_cols:]
    )
    given_rows = jnp.where(
        parity == 0, partial_value[:, :, half_cols:], partial_value[:, :, :half_cols]
    )
    got_rows, got_comb = swapped((given_rows, comb_part), "tp", 0)
    row_grad = (kept_rows.astype(jnp.float32) + got_rows.astype(jnp.float32)).astype(jnp.bfloat16)
    row_comb = (comb_part.astype(jnp.float32) + got_comb.astype(jnp.float32)).astype(jnp.bfloat16)
    back, back_comb = (
        lax.all_to_all(row_grad, ("ctx", "tp"), split_axis=0, concat_axis=0, tiled=True),
        lax.all_to_all(row_comb, ("ctx", "tp"), split_axis=0, concat_axis=0, tiled=True),
    )
    back_flat = (
        back.reshape(experts, 2, capacity, half_cols)
        .transpose(0, 2, 1, 3)
        .reshape(experts * capacity, width)
    )
    comb_flat = back_comb.reshape(experts, 2, capacity)[:, 0].reshape(-1)
    grad_in = jnp.dot(placing, back_flat, preferred_element_type=jnp.float32).astype(jnp.bfloat16)
    grad_combine = jnp.dot(chosen, comb_flat.astype(jnp.float32), precision=lax.Precision.HIGHEST)
    grad_combine = grad_combine.reshape(tok_count, top_count).astype(jnp.bfloat16)
    return (grad_in, grad_combine)


def solution(mesh):
    placed = (
        P(("ctx", "tp"), None),
        P(("ctx", "tp"), None),
        P(("ctx", "tp"), None),
        P(None, None, ("ctx", "tp")),
        P(None, None, ("ctx", "tp")),
        P(None, ("ctx", "tp")),
        P(None, ("ctx", "tp")),
        P(("ctx", "tp"), None),
    )
    return jax.shard_map(
        body,
        mesh=mesh,
        in_specs=placed,
        out_specs=(P(("ctx", "tp"), None), P(("ctx", "tp"), None)),
        check_vma=False,
    )
```

profile of v0, /device:TPU:0, one launch (start us, length us, event | category | flops | bytes accessed | tf_op | source)
XLA Modules:
  0.0 734.9 jit_solution(6042758402961175412)
XLA Ops:
  0.7 0.8 copy.83
  1.7 0.8 copy.88
  2.5 0.1 reshape.151
  2.6 1.5 reduce-window.6
  4.1 0.3 slice_reduce_fusion
  4.4 0.1 fusion.14
  4.5 0.4 broadcast_compare_fusion
  5.0 0.6 fusion.6
  5.5 0.1 copy.103
  5.7 0.7 copy.89
  6.4 11.1 %all-to-all-start.1 = ((bf16[128,1,12]{2,1,0:T(2,128)(2,1)}), bf16[128,1,12]{2,1,0:T(2,128)(2,1)S(1)}, u32[]{:S(2)}, u32[]{:S(2)}) async-start(bf16[128,1,12]{2,1,0:T(2,128)(2,1)} %copy.89), calls=%async_computation.1 | async-start | bytes 131072 | tf_op jit(solution)/shard_map/all_to_all | solution.py:44
  17.7 0.7 multiply_add_fusion.2
  18.5 0.6 convert_reduce_fusion
  19.1 4.5 convolution_convert_fusion
  23.7 9.8 %broadcast_in_dim.6 = bf16[64,12,4096]{2,1,0:T(8,128)(2,1)} reshape(bf16[768,4096]{1,0:T(8,128)(2,1)} %convolution_convert_fusion) | data formatting | bytes 12582912 | tf_op jit(solution)/shard_map/broadcast_in_dim | solution.py:36
  33.4 10.7 %broadcast_in_dim.7 = bf16[64,2,12,4096]{3,2,1,0:T(8,128)(2,1)} broadcast(bf16[64,12,4096]{2,1,0:T(8,128)(2,1)} %broadcast_in_dim.6), dimensions={0,2,3} | broadcast | bytes 18874368 | tf_op jit(solution)/shard_map/broadcast_in_dim | solution.py:36
  44.1 10.6 %all-to-all-start = ((bf16[128,12,4096]{2,1,0:T(8,128)(2,1)}), bf16[128,12,4096]{2,1,0:T(8,128)(2,1)}, u32[]{:S(2)}, u32[]{:S(2)}) async-start(bf16[128,12,4096]{2,1,0:T(8,128)(2,1)} %bitcast.49), calls=%async_computation | async-start | bytes 33554432 | tf_op jit(solution)/shard_map/all_to_all | solution.py:43
  54.7 4.0 copy.92
  58.7 6.7 reshape.150
  65.4 6.2 copy.93
  71.7 4.0 copy.90
  75.7 6.7 reshape.149
  82.4 6.1 copy.91
  88.5 0.2 convert_reduce_fusion.1
  88.7 0.1 reshape.148
  88.8 220.4 %all-to-all-done = bf16[128,12,4096]{2,1,0:T(8,128)(2,1)} async-done(((bf16[128,12,4096]{2,1,0:T(8,128)(2,1)}), bf16[128,12,4096]{2,1,0:T(8,128)(2,1)}, u32[]{:S(2)}, u32[]{:S(2)}) %all-to-all-start) | async-done | bytes 12582944 | tf_op jit(solution)/shard_map/all_to_all | solution.py:43
  309.2 18.2 %reshape.142 = bf16[1536,4096]{1,0:T(8,128)(2,1)} reshape(bf16[128,12,4096]{2,1,0:T(8,128)(2,1)} %all-to-all-done) | data formatting | bytes 25165824 | tf_op jit(solution)/shard_map/reshape | solution.py:47
  327.4 18.6 %multiply_reduce_fusion = (bf16[1536]{0:T(1024)(128)(2,1)S(1)}, f32[1536,768]{0,1:T(8,128)}) fusion(f32[1536,768]{0,1:T(8,128)} %copy.91, f32[1536,768]{0,1:T(8,128)} %copy.93, bf16[1536,4096]{1,0:T(8,128)(2,1)} %reshape.142, bf16[768,4096]{1,0:T(8,128)(2,1)} %param.15), kind=kOutput, calls=%fused_computation.4 | convolution fusion | flops 9671931904 | bytes 33033216 | tf_op jit(solution)/shard_map/dot_general | solution.py:50
  346.0 24.6 %fusion.1 = f32[1536,4096]{1,0:T(8,128)} fusion(bf16[4096,768]{1,0:T(8,128)(2,1)} %param.13, f32[1536,768]{0,1:T(8,128)} %copy.93, f32[1536,768]{0,1:T(8,128)} %copy.91, f32[1536,768]{0,1:T(8,128)} %get-tuple-element.3, f32[1536]{0:T(1024)S(1)} %reshape.148), kind=kOutput, calls=%fused_computation.10 | convolution fusion | flops 9676652544 | bytes 45619200 | tf_op jit(solution)/shard_map/dot_general | solution.py:61
  370.5 23.2 %add_convert_fusion = bf16[1536,4096]{1,0:T(8,128)(2,1)} fusion(f32[1536,4096]{1,0:T(8,128)} %fusion.1, bf16[4096,768]{1,0:T(8,128)(2,1)} %param.14, f32[1536,768]{0,1:T(8,128)} %get-tuple-element.3, f32[1536]{0:T(1024)S(1)} %reshape.148, f32[1536,768]{0,1:T(8,128)} %copy.93), kind=kOutput, calls=%fused_computation | convolution fusion | flops 9684516864 | bytes 53483520 | tf_op jit(solution)/shard_map/dot_general | solution.py:64
  393.7 17.9 %reshape.144 = bf16[128,12,4096]{2,1,0:T(8,128)(2,1)} reshape(bf16[1536,4096]{1,0:T(8,128)(2,1)} %add_convert_fusion) | data formatting | bytes 25165824 | tf_op jit(solution)/shard_map/reshape | solution.py:67
  411.6 6.5 broadcast_select_fusion
  418.1 6.1 copy.96
  424.3 0.1 convert_element_type.107
  424.4 2.1 collective-permute-start.1
  426.5 135.4 %collective-permute-done.1 = bf16[128,12]{1,0:T(8,128)(2,1)S(1)} collective-permute-done((bf16[128,12]{1,0:T(8,128)(2,1)S(1)}, bf16[128,12]{1,0:T(8,128)(2,1)S(1)}, u32[]{:S(2)}, u32[]{:S(2)}) %collective-permute-start.1) | collective-permute-done | bytes 3104 | tf_op jit(solution)/shard_map/ppermute | solution.py:8
  561.9 0.7 copy.101
  562.6 17.9 %all-to-all-start.3 = ((bf16[128,1,12]{2,1,0:T(2,128)(2,1)}), bf16[128,1,12]{2,1,0:T(2,128)(2,1)S(1)}, u32[]{:S(2)}, u32[]{:S(2)}) async-start(bf16[128,1,12]{2,1,0:T(2,128)(2,1)} %copy.101), calls=%async_computation.3 | async-start | bytes 131072 | tf_op jit(solution)/shard_map/all_to_all | solution.py:80
  580.5 14.0 %add_convert_fusion.1 = bf16[128,12,2048]{2,1,0:T(8,128)(2,1)} fusion(bf16[128,12,2048]{2,0,1:T(8,128)(2,1)} %collective-permute-done, pred[]{:T(512)S(6)} %eq.100, bf16[128,12,4096]{2,1,0:T(8,128)(2,1)} %reshape.144), kind=kLoop, calls=%fused_computation.1 | loop fusion | flops 15728640 | bytes 25165824 | tf_op jit(solution)/shard_map/convert_element_type | solution.py:76
  594.5 10.5 %all-to-all-start.2 = ((bf16[128,12,2048]{2,1,0:T(8,128)(2,1)}), bf16[128,12,2048]{2,1,0:T(8,128)(2,1)}, u32[]{:S(2)}, u32[]{:S(2)}) async-start(bf16[128,12,2048]{2,1,0:T(8,128)(2,1)} %add_convert_fusion.1), calls=%async_computation.2 | async-start | bytes 16777216 | tf_op jit(solution)/shard_map/all_to_all | solution.py:79
  605.0 0.1 slice_reduce_fusion.1
  605.1 0.1 reshape.153
  605.2 2.3 fusion.8
  607.6 0.7 copy.104
  608.2 107.1 %all-to-all-done.2 = bf16[128,12,2048]{2,1,0:T(8,128)(2,1)} async-done(((bf16[128,12,2048]{2,1,0:T(8,128)(2,1)}), bf16[128,12,2048]{2,1,0:T(8,128)(2,1)}, u32[]{:S(2)}, u32[]{:S(2)}) %all-to-all-start.2) | async-done | bytes 6291488 | tf_op jit(solution)/shard_map/all_to_all | solution.py:79
  715.4 13.1 %copy.98 = bf16[64,2,12,2048]{3,1,2,0:T(2,128)(2,1)S(1)} copy(bf16[64,2,12,2048]{3,2,1,0:T(8,128)(2,1)} %bitcast.4) | data formatting | bytes 12582912 | tf_op jit(solution)/shard_map/reshape | solution.py:83
  728.5 4.0 copy.107
  732.5 2.1 convolution_convert_fusion.1
  (24 shorter events, 0.5 us)
Async XLA Ops:
  0.6 18.5 %copy-start = (bf16[80,4096]{1,0:T(8,128)(2,1)S(1)}, bf16[80,4096]{1,0:T(8,128)(2,1)}, u32[]{:S(2)}) copy-start(bf16[80,4096]{1,0:T(8,128)(2,1)} %param.8) | copy-start | bytes 1966084
  6.4 27.1 %all-to-all-start.1 = ((bf16[128,1,12]{2,1,0:T(2,128)(2,1)}), bf16[128,1,12]{2,1,0:T(2,128)(2,1)S(1)}, u32[]{:S(2)}, u32[]{:S(2)}) async-start(bf16[128,1,12]{2,1,0:T(2,128)(2,1)} %copy.89), calls=%async_computation.1 | async-start | bytes 131072 | tf_op jit(solution)/shard_map/all_to_all | solution.py:44
  44.1 10.6 %copy-start.2 = (bf16[128,12,768]{2,0,1:T(8,128)(2,1)S(1)}, bf16[128,12,768]{2,0,1:T(8,128)(2,1)}, u32[]{:S(2)}) copy-start(bf16[128,12,768]{2,0,1:T(8,128)(2,1)} %param.11) | copy-start | bytes 7077892
  44.1 265.1 %all-to-all-start = ((bf16[128,12,4096]{2,1,0:T(8,128)(2,1)}), bf16[128,12,4096]{2,1,0:T(8,128)(2,1)}, u32[]{:S(2)}, u32[]{:S(2)}) async-start(bf16[128,12,4096]{2,1,0:T(8,128)(2,1)} %bitcast.49), calls=%async_computation | async-start | bytes 33554432 | tf_op jit(solution)/shard_map/all_to_all | solution.py:43
  65.4 6.2 copy-start.3
  424.3 156.2 %collective-permute-start = (bf16[128,12,2048]{2,0,1:T(8,128)(2,1)}, bf16[128,12,2048]{2,0,1:T(8,128)(2,1)}, u32[]{:S(2)}, u32[]{:S(2)}) collective-permute-start(bf16[128,12,2048]{2,0,1:T(8,128)(2,1)} %copy.96), channel_id=1, source_target_pairs={{0,1},{1,0},{2,3},{3,2},{4,5},{5,4},{6,7},{7,6},{8,9},{9,8},{10,11... | collective-permute-start | bytes 18874376 | tf_op jit(solution)/shard_map/ppermute | solution.py:8
  424.4 137.5 %collective-permute-start.1 = (bf16[128,12]{1,0:T(8,128)(2,1)S(1)}, bf16[128,12]{1,0:T(8,128)(2,1)S(1)}, u32[]{:S(2)}, u32[]{:S(2)}) collective-permute-start(bf16[128,12]{1,0:T(8,128)(2,1)S(1)} %convert_element_type.107), channel_id=1, source_target_pairs={{0,1},{1,0},{2,3},{3,2},{4,5},{5,4},{6,7},{7,6},{8,9},{9,8},{10,11... | collective-permute-start | bytes 9224 | tf_op jit(solution)/shard_map/ppermute | solution.py:8
  562.6 31.9 %all-to-all-start.3 = ((bf16[128,1,12]{2,1,0:T(2,128)(2,1)}), bf16[128,1,12]{2,1,0:T(2,128)(2,1)S(1)}, u32[]{:S(2)}, u32[]{:S(2)}) async-start(bf16[128,1,12]{2,1,0:T(2,128)(2,1)} %copy.101), calls=%async_computation.3 | async-start | bytes 131072 | tf_op jit(solution)/shard_map/all_to_all | solution.py:80
  594.5 120.9 %all-to-all-start.2 = ((bf16[128,12,2048]{2,1,0:T(8,128)(2,1)}), bf16[128,12,2048]{2,1,0:T(8,128)(2,1)}, u32[]{:S(2)}, u32[]{:S(2)}) async-start(bf16[128,12,2048]{2,1,0:T(8,128)(2,1)} %add_convert_fusion.1), calls=%async_computation.2 | async-start | bytes 16777216 | tf_op jit(solution)/shard_map/all_to_all | solution.py:79
  728.5 6.2 copy-start.1
where the time goes:
time: 748 us; the launch traced here: 735 us
  waiting for transfers between devices  463 us (62%)
  local copies, waits for them, and re-layouts  119 us (16%)
  matrix products  75.9 us (10%)
  starting transfers between devices  52.2 us (7%)
  other arithmetic  24.2 us (3%)
    all_to_all x1, waiting for transfers between devices, body(): lax.all_to_all(send_rows, ('ctx', 'tp'), split_axis=0, concat_axis=0, til...  220 us
    ppermute x2, waiting for transfers between devices, swapped(): lax.ppermute(value, axis, [(i, i ^ 1 << stride) for i in range(lax.axis_s...  135 us
    all_to_all x1, waiting for transfers between devices, body(): lax.all_to_all(row_grad, ('ctx', 'tp'), split_axis=0, concat_axis=0, tile...  107 us
    dot_general x1, matrix products, body(): lax.dot_general(dgate, gate_weight, (((1,), (1,)), ((), ())), preferred_e...  24.6 us
    dot_general x1, matrix products, body(): lax.dot_general(dup, up_weight, (((1,), (1,)), ((), ())), preferred_eleme...  23.2 us
    broadcast_in_dim x2, local copies, waits for them, and re-layouts, body(): jnp.broadcast_to(outbound.reshape(experts, 1, capacity, width), (experts,...  20.5 us
    dot_general x1, matrix products, body(): lax.dot_general(grad_rows, down_weight, (((1,), (1,)), ((), ())), preferr...  18.6 us
    reshape x1, local copies, waits for them, and re-layouts, body(): grad_rows = arrived.reshape(row_count, width)  18.2 us
  transfers between devices with their start and end apart: 6, of which 3 were waited for; matrix products, arithmetic and copies ran while one was open for 9% of the time, Pallas kernels for 0%

commit v1 on v0

v1 whole, which is shorter than its diff:
```python
import functools

import jax
import jax.numpy as jnp
from jax import lax
from jax.experimental import pallas as pl
from jax.experimental.pallas import tpu as pltpu
from jax.sharding import PartitionSpec as P

MESH = pl.DeviceIdType.MESH
FLIPS = (0, 1, 2, 4, 3, 5, 6, 7)
BF = jnp.bfloat16
F32 = jnp.float32
NT = (((1,), (1,)), ((), ()))


def bits(f):
    return f & 1, (f >> 1) & 1, (f >> 2) & 1


def outer(v, c):
    return (v + 3 + 2 * ((v + c) % 2)) % 4


def inner(v, c):
    return (v + 1 + 2 * ((v + c) % 2)) % 4


def flipped(xyz, f, c, how):
    return tuple(how(v, c) if b else v for v, b in zip(xyz, bits(f)))


def device(xyz, c):
    x, y, z = xyz
    return ((y // 2 * 4 + z) * 2 + c, (y % 2) * 4 + x)


def expert_of(xyz, c):
    ctx, tp = device(xyz, c)
    return ctx * 4 + tp // 2


def iota(shape, dim):
    return lax.broadcasted_iota(jnp.int32, shape, dim).astype(F32)


def kernel(
    tokens, slots, width, hidden,
    grad_ref, ids_ref, comb_ref, gate_hbm, up_hbm, gw_hbm, uw_hbm, dw_hbm,
    out_ref, outc_ref, recv, ret,
    tok, stage, gw, uw, dw, sav_g, sav_u, gf, uf, dg, du, cacc, gb, rc, sel, selp, selw, plac, wplac, part,
    w_sem, s_sem, l_sem, tok_send, tok_recv, dis_send, dis_recv, ret_send, ret_recv, part_send, part_recv,
):
    ext = 128
    full = width + ext
    half = 4 * slots
    msg = 2 * half
    cover = 16 * half
    ctx, tp = lax.axis_index("ctx"), lax.axis_index("tp")
    c = ctx % 2
    me = (tp % 4, ctx // 8 * 2 + tp // 4, ctx // 2 % 4)
    mbit = tuple((v + c) % 2 for v in me)
    mine = mbit[2] * 4 + mbit[1] * 2 + mbit[0]
    my_expert = expert_of(me, c)

    def member(r):
        b = tuple(1 - v if t else v for v, t in zip(mbit, bits(r)))
        return b[2] * 4 + b[1] * 2 + b[0]

    def rows(start, size):
        return pl.ds(pl.multiple_of(start, 16), size)

    w_copies = [
        pltpu.make_async_copy(a, b, w_sem.at[i])
        for i, (a, b) in enumerate(((dw_hbm, dw), (gw_hbm, gw), (uw_hbm, uw)))
    ]
    for copy in w_copies:
        copy.start()

    def saved_copies(k, q, m):
        p, sc = 2 * k + q // 2, q % 2
        sender = flipped(me, FLIPS[p], sc, outer)
        mb = (m % 2, m // 2 % 2, m // 4)
        src = tuple((v - (v + sc) % 2 + b + 4) % 4 for v, b in zip(sender, mb))
        sctx, stp = device(src, sc)
        s = sctx * 8 + stp
        at = q * 8 + m
        return (
            pltpu.make_async_copy(gate_hbm.at[s], sav_g.at[at], s_sem.at[0, at]),
            pltpu.make_async_copy(up_hbm.at[s], sav_u.at[at], s_sem.at[1, at]),
        )

    def saved_start(k):
        for q in range(4):
            @pl.loop(0, 8)
            def _(m):
                for copy in saved_copies(k, q, m):
                    copy.start()

    def saved_wait(k):
        for q in range(4):
            @pl.loop(0, 8)
            def _(m):
                for copy in saved_copies(k, q, m):
                    copy.wait()

    saved_start(0)

    barrier = pltpu.get_barrier_semaphore()
    friends = [device(me, 1 - c)]
    for f in range(1, 8):
        friends.append(device(flipped(me, f, c, outer), c))
        friends.append(device(flipped(me, f, c, outer), 1 - c))
        friends.append(device(flipped(me, f, 1 - c, outer), 1 - c))
        friends.append(device(flipped(me, f, c, inner), c))
    for friend in friends:
        pl.semaphore_signal(barrier, inc=1, device_id=friend, device_id_type=MESH)

    own = rows(mine * tokens, tokens)
    tok[own, 0:width] = grad_ref[...]
    lane = lax.broadcasted_iota(jnp.int32, (tokens, ext), 1)
    lane64 = jnp.where(lane >= 64, lane - 64, lane)
    ids = ids_ref[...]
    combine = comb_ref[...].astype(F32)
    hot = jnp.zeros((tokens, ext), F32)
    weight = jnp.zeros((tokens, ext), F32)
    for k in range(ids.shape[1]):
        same = ids[:, k : k + 1] == lane64
        hot = jnp.where(same, 1.0, hot)
        weight = jnp.where(same, combine[:, k : k + 1], weight)
    lower = (iota((tokens, tokens), 1) < iota((tokens, tokens), 0)).astype(F32).astype(BF)
    count = jnp.dot(lower, hot.astype(BF), preferred_element_type=F32)
    table = jnp.where(lane < 64, jnp.where(hot > 0.5, count, -1.0), weight)
    tok[own, width:full] = table.astype(BF)

    pl.semaphore_wait(barrier, len(friends))

    def tok_copy(r):
        return pltpu.make_async_remote_copy(
            src_ref=tok.at[own],
            dst_ref=tok.at[own],
            send_sem=tok_send.at[r],
            recv_sem=tok_recv.at[r],
            device_id=device(flipped(me, r, c, inner), c),
            device_id_type=MESH,
        )

    def tok_arrival(r):
        there = rows(member(r) * tokens, tokens)
        return pltpu.make_async_remote_copy(
            src_ref=tok.at[there],
            dst_ref=tok.at[there],
            send_sem=tok_send.at[r],
            recv_sem=tok_recv.at[r],
            device_id=device(flipped(me, r, c, inner), c),
            device_id_type=MESH,
        )

    for r in range(1, 8):
        tok_copy(r).start()

    slane = lax.broadcasted_iota(jnp.int32, (half, ext), 1)
    for i in range(16):
        e = expert_of(flipped(me, FLIPS[i // 2], c, outer), i % 2)
        selp[i * half : (i + 1) * half, :] = jnp.where(slane == e, 1.0, 0.0).astype(BF)
        selw[i * half : (i + 1) * half, :] = jnp.where(slane == e + 64, 1.0, 0.0).astype(BF)

    def slot_of(j):
        block = jnp.floor((j + 0.5) * (1.0 / slots))
        group = jnp.floor((block + 0.5) * 0.25)
        return j - block * slots, block - group * 4

    def owner_of(t):
        return jnp.floor((t + 0.5) * (1.0 / tokens))

    def dis_copy(i, h, p, dc):
        here = rows(i * msg + h * half, half)
        there = rows((2 * p + c) * msg + h * half, half)
        dst = device(flipped(me, FLIPS[p], c, outer), dc)
        return pltpu.make_async_remote_copy(
            src_ref=stage.at[here, pl.ds(0, width)],
            dst_ref=recv.at[there],
            send_sem=dis_send.at[i * 2 + h],
            recv_sem=dis_recv.at[(2 * p + c) * 2 + h],
            device_id=dst,
            device_id_type=MESH,
        )

    def dis_self(h):
        here = rows(c * msg + h * half, half)
        return pltpu.make_async_copy(stage.at[here, pl.ds(0, width)], recv.at[here], l_sem.at[h])

    def dis_arrival(j, h):
        here = rows(j * msg + h * half, half)
        return pltpu.make_async_remote_copy(
            src_ref=stage.at[here, pl.ds(0, width)],
            dst_ref=recv.at[here],
            send_sem=dis_send.at[j * 2 + h],
            recv_sem=dis_recv.at[j * 2 + h],
            device_id=device(me, 1 - c),
            device_id_type=MESH,
        )

    for step in range(2):
        h = mbit[2] if step == 0 else 1 - mbit[2]
        for r in range(4 * step, 4 * step + 4):
            if r > 0:
                tok_arrival(r).wait_recv()
        there = rows(h * 4 * tokens, 4 * tokens)
        tables = tok[there, width:full]
        pos = lax.dot_general(selp[...], tables, NT, preferred_element_type=F32)
        slot, four = slot_of(iota((cover, 1), 0))
        owner = owner_of(iota((1, 4 * tokens), 1))
        sel[...] = jnp.where((pos == slot) & (four == owner), 1.0, 0.0).astype(BF)

        tile = 512

        @pl.loop(0, width // tile)
        def _(n):
            cols = pl.ds(pl.multiple_of(n * tile, tile), tile)
            got = jnp.dot(sel[...], tok[there, cols], preferred_element_type=F32).astype(BF)
            for i in range(16):
                stage[rows(i * msg + h * half, half), cols] = got[i * half : (i + 1) * half]

        dis_self(h).start()
        dis_copy(1 - c, h, 0, 1 - c).start()
        for p in range(1, 8):
            for dc in range(2):
                dis_copy(2 * p + dc, h, p, dc).start()

    slot, four = slot_of(iota((1, cover), 1))
    owner = owner_of(iota((4 * tokens, 1), 0))
    for h in range(2):
        tables = tok[h * 4 * tokens : (h + 1) * 4 * tokens, width:full]
        pos = lax.dot_general(tables, selp[...], NT, preferred_element_type=F32)
        wgt = lax.dot_general(tables, selw[...], NT, preferred_element_type=F32)
        hit = (pos == slot) & (four == owner)
        plac[h] = jnp.where(hit, 1.0, 0.0).astype(BF)
        wplac[h] = jnp.where(hit, wgt, 0.0).astype(BF)

    for copy in w_copies:
        copy.wait()

    def ret_copy(j, h, p, dc):
        here = rows(j * msg + h * half, half)
        there = rows((2 * p + c) * half, half)
        return pltpu.make_async_remote_copy(
            src_ref=stage.at[here],
            dst_ref=ret.at[h, there],
            send_sem=ret_send.at[j * 2 + h],
            recv_sem=ret_recv.at[(2 * p + c) * 2 + h],
            device_id=device(flipped(me, FLIPS[p], dc, outer), dc),
            device_id_type=MESH,
        )

    def ret_self(h):
        here = rows(c * msg + h * half, half)
        return pltpu.make_async_copy(stage.at[here], ret.at[h, rows(c * half, half)], l_sem.at[2 + h])

    def ret_arrival(j, h):
        return pltpu.make_async_remote_copy(
            src_ref=stage.at[rows(j * msg + h * half, half)],
            dst_ref=ret.at[h, rows(j * half, half)],
            send_sem=ret_send.at[j * 2 + h],
            recv_sem=ret_recv.at[j * 2 + h],
            device_id=device(me, 1 - c),
            device_id_type=MESH,
        )

    batch = 4 * msg
    elane = lax.broadcasted_iota(jnp.int32, (batch, ext), 1)
    for k in range(4):
        saved_wait(k)

        @pl.loop(0, 16)
        def _(i):
            pair = pl.ds(pl.multiple_of(i * 2 * slots, 8), 2 * slots)
            for src, dst in ((sav_g, gf), (sav_u, uf)):
                dst[pair, :] = jnp.concatenate(
                    [src[2 * i].astype(F32), src[2 * i + 1].astype(F32)], axis=0
                )

        if k < 3:
            saved_start(k + 1)
        for j in range(4 * k, 4 * k + 4):
            if j >= 2:
                for h in range(2):
                    dis_arrival(j, h).wait_recv()
        if k == 0:
            for h in range(2):
                dis_arrival(1 - c, h).wait_recv()
                dis_self(h).wait()
        buf = gb.at[pl.ds((k % 2) * batch, batch)]
        load = pltpu.make_async_copy(recv.at[pl.ds(k * batch, batch)], buf, l_sem.at[4])
        load.start()
        load.wait()

        cacc[...] = jnp.zeros_like(cacc)
        tile = 256

        @pl.loop(0, hidden // tile)
        def _(n):
            cols = pl.ds(pl.multiple_of(n * tile, tile), tile)
            dh = lax.dot_general(buf[...], dw[cols, :], NT, preferred_element_type=F32)
            g, u = gf[:, cols], uf[:, cols]
            sg = jax.nn.sigmoid(g)
            a = g * sg
            prod = a * u * dh
            total = cacc[...]
            for b in range(tile // ext):
                total = total + prod[:, b * ext : (b + 1) * ext]
            cacc[...] = total
            dg[:, cols] = (dh * u * sg * (1.0 + g * (1.0 - sg))).astype(BF)
            du[:, cols] = (dh * a).astype(BF)

        for j in range(4 * k, 4 * k + 4):
            if j >= 2:
                for h in range(2):
                    dis_copy(j, h, j // 2, j % 2).wait_send()
        if k == 0:
            for h in range(2):
                dis_copy(1 - c, h, 0, 1 - c).wait_send()

        here = pl.ds(k * batch, batch)
        comb = jnp.sum(cacc[...], axis=1, keepdims=True)
        stage[here, width:full] = jnp.where(elane == my_expert, comb, 0.0).astype(BF)
        xtile = 512

        @pl.loop(0, width // xtile)
        def _(n):
            cols = pl.ds(pl.multiple_of(n * xtile, xtile), xtile)
            x = lax.dot_general(dg[...], gw[cols, :], NT, preferred_element_type=F32)
            x = x + lax.dot_general(du[...], uw[cols, :], NT, preferred_element_type=F32)
            stage[here, cols] = x.astype(BF)

        if k == 0:
            for h in range(2):
                ret_self(h).start()
                ret_copy(1 - c, h, 0, 1 - c).start()
        for j in range(4 * k, 4 * k + 4):
            if j >= 2:
                for h in range(2):
                    ret_copy(j, h, j // 2, j % 2).start()

    for r in range(1, 8):
        tok_copy(r).wait_send()

    def part_copy(r):
        return pltpu.make_async_remote_copy(
            src_ref=tok.at[rows(member(r) * tokens, tokens)],
            dst_ref=part.at[pl.ds(r * tokens, tokens)],
            send_sem=part_send.at[r],
            recv_sem=part_recv.at[r],
            device_id=device(flipped(me, r, c, inner), c),
            device_id_type=MESH,
        )

    for step in range(2):
        h = 1 - mbit[2] if step == 0 else mbit[2]
        for j in range(2, 16):
            ret_arrival(j, h).wait_recv()
        ret_arrival(1 - c, h).wait_recv()
        ret_self(h).wait()
        loads = (
            pltpu.make_async_copy(ret.at[h, :, pl.ds(0, width)], gb, l_sem.at[5]),
            pltpu.make_async_copy(ret.at[h, :, pl.ds(width, ext)], rc, l_sem.at[6]),
        )
        for load in loads:
            load.start()
        for load in loads:
            load.wait()
        there = rows(h * 4 * tokens, 4 * tokens)
        tok[there, width:full] = jnp.dot(plac[h], rc[...], preferred_element_type=F32).astype(BF)
        tile = 512

        @pl.loop(0, width // tile)
        def _(n):
            cols = pl.ds(pl.multiple_of(n * tile, tile), tile)
            tok[there, cols] = jnp.dot(wplac[h], gb[:, cols], preferred_element_type=F32).astype(BF)

        for r in range(4 - 4 * step, 8 - 4 * step):
            if r > 0:
                part_copy(r).start()

    for r in range(1, 8):
        part_copy(r).wait_recv()
    tile = 512

    @pl.loop(0, width // tile)
    def _(n):
        cols = pl.ds(pl.multiple_of(n * tile, tile), tile)
        total = tok[own, cols].astype(F32)
        for r in range(1, 8):
            total = total + part[r * tokens : (r + 1) * tokens, cols].astype(F32)
        out_ref[:, cols] = total.astype(BF)

    total = tok[own, width:full].astype(F32)
    for r in range(1, 8):
        total = total + part[r * tokens : (r + 1) * tokens, width:full].astype(F32)
    total = jnp.where(lane < 64, total, 0.0)
    klane = lax.broadcasted_iota(jnp.int32, ids.shape, 1)
    result = jnp.zeros(ids.shape, F32)
    for k in range(ids.shape[1]):
        value = jnp.sum(jnp.where(ids[:, k : k + 1] == lane, total, 0.0), axis=1, keepdims=True)
        result = jnp.where(klane == k, value, result)
    outc_ref[...] = result.astype(BF)

    for r in range(1, 8):
        part_copy(r).wait_send()
    for h in range(2):
        ret_copy(1 - c, h, 0, 1 - c).wait_send()
        for j in range(2, 16):
            ret_copy(j, h, j // 2, j % 2).wait_send()


def body(grad_out, expert_ids, combine, gate_saved, up_saved, gate_weight, up_weight, down_weight):
    tokens, width = grad_out.shape
    sources, slots, hidden = gate_saved.shape
    top = expert_ids.shape[1]
    full = width + 128
    half = 4 * slots
    cover = 16 * half
    batch = 8 * half
    vmem = pl.BlockSpec(memory_space=pltpu.VMEM)
    hbm = pl.BlockSpec(memory_space=pl.ANY)
    dma = pltpu.SemaphoreType.DMA
    out = pl.pallas_call(
        functools.partial(kernel, tokens, slots, width, hidden),
        out_shape=(
            jax.ShapeDtypeStruct((tokens, width), BF),
            jax.ShapeDtypeStruct((tokens, top), BF),
            jax.ShapeDtypeStruct((2 * cover, width), BF),
            jax.ShapeDtypeStruct((2, cover, full), BF),
        ),
        in_specs=[vmem, vmem, vmem, hbm, hbm, hbm, hbm, hbm],
        out_specs=(vmem, vmem, hbm, hbm),
        scratch_shapes=[
            pltpu.VMEM((8 * tokens, full), BF),
            pltpu.VMEM((2 * cover, full), BF),
            pltpu.VMEM((width, hidden), BF),
            pltpu.VMEM((width, hidden), BF),
            pltpu.VMEM((hidden, width), BF),
            pltpu.VMEM((32, slots, hidden), BF),
            pltpu.VMEM((32, slots, hidden), BF),
            pltpu.VMEM((batch, hidden), F32),
            pltpu.VMEM((batch, hidden), F32),
            pltpu.VMEM((batch, hidden), BF),
            pltpu.VMEM((batch, hidden), BF),
            pltpu.VMEM((batch, 128), F32),
            pltpu.VMEM((cover, width), BF),
            pltpu.VMEM((cover, 128), BF),
            pltpu.VMEM((cover, 4 * tokens), BF),
            pltpu.VMEM((cover, 128), BF),
            pltpu.VMEM((cover, 128), BF),
            pltpu.VMEM((2, 4 * tokens, cover), BF),
            pltpu.VMEM((2, 4 * tokens, cover), BF),
            pltpu.VMEM((8 * tokens, full), BF),
            dma((3,)),
            dma((2, 32)),
            dma((7,)),
            dma((8,)),
            dma((8,)),
            dma((32,)),
            dma((32,)),
            dma((32,)),
            dma((32,)),
            dma((8,)),
            dma((8,)),
        ],
        compiler_params=pltpu.CompilerParams(
            collective_id=0, has_side_effects=True, vmem_limit_bytes=66 * 1000 * 1000
        ),
        cost_estimate=pl.CostEstimate(
            flops=6 * sources * slots * hidden * width,
            bytes_accessed=80_000_000,
            transcendentals=sources * slots * hidden,
        ),
    )(grad_out, expert_ids, combine, gate_saved, up_saved, gate_weight, up_weight, down_weight)
    return out[0], out[1]


def solution(mesh):
    placed = (
        P(("ctx", "tp"), None),
        P(("ctx", "tp"), None),
        P(("ctx", "tp"), None),
        P(None, None, ("ctx", "tp")),
        P(None, None, ("ctx", "tp")),
        P(None, ("ctx", "tp")),
        P(None, ("ctx", "tp")),
        P(("ctx", "tp"), None),
    )
    return jax.shard_map(
        body,
        mesh=mesh,
        in_specs=placed,
        out_specs=(P(("ctx", "tp"), None), P(("ctx", "tp"), None)),
        check_vma=False,
    )
```

time: 748 us -> 272 us (0.36); the launches traced: 735 us -> 271 us
  waiting for transfers between devices: 463 us -> 0 us
  Pallas kernels: 0 us -> 256 us
  local copies, waits for them, and re-layouts: 119 us -> 14 us
  matrix products: 75.9 us -> 0 us
  starting transfers between devices: 52.2 us -> 0 us
  other arithmetic: 24.2 us -> 0 us
    all_to_all x4 -> x0, waiting for transfers between devices: 328 us -> none  [the longest x1 220 us: body(): lax.all_to_all(send_rows, ('ctx', 'tp'), split_axis=0, concat_axis=0, til...]
    pallas_call x0 -> x1, Pallas kernels: none -> 256 us  [body(): pl.pallas_call(functools.partial(kernel, tokens, slots, width, hidden), o...]
    ppermute x2 -> x0, waiting for transfers between devices: 135 us -> none  [swapped(): lax.ppermute(value, axis, [(i, i ^ 1 << stride) for i in range(lax.axis_s...]
    dot_general x7 -> x0, matrix products: 75.9 us -> none  [the longest x1 24.6 us: body(): lax.dot_general(dgate, gate_weight, (((1,), (1,)), ((), ())), preferred_e...]
    all_to_all x4 -> x0, starting transfers between devices: 50.1 us -> none  [the longest x1 17.9 us: body(): lax.all_to_all(row_comb, ('ctx', 'tp'), split_axis=0, concat_axis=0, tile...]
    reshape x3 -> x0, local copies, waits for them, and re-layouts: 49.2 us -> none  [the longest x1 18.2 us: body(): grad_rows = arrived.reshape(row_count, width)]
    convert_element_type x8 -> x0, local copies, waits for them, and re-layouts: 34 us -> none  [the longest x3 16.9 us: body(): gate_pre = gate_saved.reshape(row_count, half_width).astype(jnp.float32)]
    broadcast_in_dim x3 -> x0, local copies, waits for them, and re-layouts: 20.5 us -> none  [the longest x2 20.5 us: body(): jnp.broadcast_to(outbound.reshape(experts, 1, capacity, width), (experts,...]
  transfers between devices with their start and end apart: 6 -> 0, of which waited for: 3 -> 0; matrix products, arithmetic and copies ran while one was open for 9% -> 0% of each run, Pallas kernels for 0% -> 0%
where the time goes in v1:
time: 272 us; the launch traced here: 271 us
  Pallas kernels  256 us (94%)
  local copies, waits for them, and re-layouts  14 us (5%)
    pallas_call x1, Pallas kernels, body(): pl.pallas_call(functools.partial(kernel, tokens, slots, width, hidden), o...  256 us
    unnamed x8, local copies, waits for them, and re-layouts  14 us

profile of v1, /device:TPU:0, one launch (start us, length us, event | category | flops | bytes accessed | tf_op | source)
XLA Modules:
  0.0 271.1 jit_solution(18310801104602350891)
XLA Ops:
  0.6 0.0 copy-start
  0.6 1.5 copy.11.comb_ref
  2.2 1.4 copy.10.ids_ref
  3.6 4.7 %copy.12.gate_hbm = bf16[128,12,768]{2,1,0:T(8,128)(2,1)} copy(bf16[128,12,768]{2,0,1:T(8,128)(2,1)} %param.11) | data formatting | bytes 4718592 | tf_op args[3]
  8.3 0.0 copy-done
  8.3 3.1 %copy.13.up_hbm = bf16[128,12,768]{2,1,0:T(8,128)(2,1)} copy(bf16[128,12,768]{2,0,1:T(8,128)(2,1)S(1)} %copy-done) | data formatting | bytes 4718592 | tf_op args[4]
  11.3 256.5 %shard_map.95 = (bf16[80,4096]{1,0:T(8,128)(2,1)}, bf16[80,8]{1,0:T(8,128)(2,1)}, bf16[1536,4096]{1,0:T(8,128)(2,1)}, bf16[2,768,4224]{2,1,0:T(8,128)(2,1)}) custom-call(bf16[80,4096]{1,0:T(8,128)(2,1)} %grad_ref.1, s32[80,8]{1,0:T(8,128)} %copy.10.ids_ref, bf16[80,8]{1,0:T(8,128)(2,1)} %copy.11.comb_ref, bf16[128,12,768]{2,1,0:T(8,128)(2,1)} %copy.12.gate_hbm, ...), custom_call_target="tpu_custom_call" | custom-call | flops 28991029248 | bytes 80000000 | tf_op jit(solution)/shard_map/pallas_call | solution.py:427
  267.8 1.4 copy.14
  269.2 2.0 copy.16
Async XLA Ops:
  0.6 7.6 %copy-start = (bf16[128,12,768]{2,0,1:T(8,128)(2,1)S(1)}, bf16[128,12,768]{2,0,1:T(8,128)(2,1)}, u32[]{:S(2)}) copy-start(bf16[128,12,768]{2,0,1:T(8,128)(2,1)} %param.12) | copy-start | bytes 7077892

commit v2 on v1

--- a/solution.py
+++ b/solution.py
@@ -8,7 +8,7 @@
 from jax.sharding import PartitionSpec as P
 
 MESH = pl.DeviceIdType.MESH
-FLIPS = (0, 1, 2, 4, 3, 5, 6, 7)
+FLIPS = (0, 7, 1, 6, 2, 5, 3, 4)
 BF = jnp.bfloat16
 F32 = jnp.float32
 NT = (((1,), (1,)), ((), ()))
@@ -48,8 +48,8 @@
     tokens, slots, width, hidden,
     grad_ref, ids_ref, comb_ref, gate_hbm, up_hbm, gw_hbm, uw_hbm, dw_hbm,
     out_ref, outc_ref, recv, ret,
-    tok, stage, gw, uw, dw, sav_g, sav_u, gf, uf, dg, du, cacc, gb, rc, sel, selp, selw, plac, wplac, part,
-    w_sem, s_sem, l_sem, tok_send, tok_recv, dis_send, dis_recv, ret_send, ret_recv, part_send, part_recv,
+    tok, stage, gw, uw, dw, sav_g, sav_u, gf, uf, dg, du, perm, cacc, gb, rc, sel, selp, selw, plac, wplac, part,
+    w_sem, l_sem, tok_send, tok_recv, dis_send, dis_recv, ret_send, ret_recv, part_send, part_recv,
 ):
     ext = 128
     full = width + ext
@@ -77,34 +77,41 @@
     for copy in w_copies:
         copy.start()
 
-    def saved_copies(k, q, m):
-        p, sc = 2 * k + q // 2, q % 2
-        sender = flipped(me, FLIPS[p], sc, outer)
-        mb = (m % 2, m // 2 % 2, m // 4)
-        src = tuple((v - (v + sc) % 2 + b + 4) % 4 for v, b in zip(sender, mb))
-        sctx, stp = device(src, sc)
-        s = sctx * 8 + stp
-        at = q * 8 + m
-        return (
-            pltpu.make_async_copy(gate_hbm.at[s], sav_g.at[at], s_sem.at[0, at]),
-            pltpu.make_async_copy(up_hbm.at[s], sav_u.at[at], s_sem.at[1, at]),
-        )
-
-    def saved_start(k):
+    s_copies = [
+        pltpu.make_async_copy(a, b, w_sem.at[3 + i])
+        for i, (a, b) in enumerate(((gate_hbm, sav_g), (up_hbm, sav_u)))
+    ]
+    for copy in s_copies:
+        copy.start()
+
+    def source_parts(sender, sc):
+        out = []
+        for v, part_of in zip(
+            sender, (lambda x: x, lambda y: y // 2 * 64 + y % 2 * 4, lambda z: z * 16)
+        ):
+            low = v - (v + sc) % 2 + 4
+            out.append((part_of(low % 4), part_of((low + 1) % 4)))
+        return out
+
+    def permute_saved(k):
+        r = iota((msg, 1), 0)
+        m = jnp.floor((r + 0.5) * (1.0 / slots))
+        slot = r - m * slots
+        mz = jnp.floor((m + 0.5) * 0.25)
+        my = jnp.floor((m - 4 * mz + 0.5) * 0.5)
+        mx = m - 4 * mz - 2 * my
+        lanes = iota((1, cover * 2), 1)
         for q in range(4):
-            @pl.loop(0, 8)
-            def _(m):
-                for copy in saved_copies(k, q, m):
-                    copy.start()
-
-    def saved_wait(k):
-        for q in range(4):
-            @pl.loop(0, 8)
-            def _(m):
-                for copy in saved_copies(k, q, m):
-                    copy.wait()
-
-    saved_start(0)
+            p, sc = 2 * k + q // 2, q % 2
+            parts = source_parts(flipped(me, FLIPS[p], sc, outer), sc)
+            at = slot * (cover * 2 // slots) + 8.0 * sc
+            for bit, (low, high) in zip((mx, my, mz), parts):
+                at = at + jnp.where(bit > 0.5, high.astype(F32), low.astype(F32))
+            perm[q * msg : (q + 1) * msg, :] = jnp.where(at == lanes, 1.0, 0.0).astype(BF)
+        for src, dst in ((sav_g, gf), (sav_u, uf)):
+            for n in range(hidden // 256):
+                cols = slice(n * 256, (n + 1) * 256)
+                dst[:, cols] = jnp.dot(perm[...], src[:, cols], preferred_element_type=F32).astype(BF)
 
     barrier = pltpu.get_barrier_semaphore()
     friends = [device(me, 1 - c)]
@@ -118,22 +125,28 @@
 
     own = rows(mine * tokens, tokens)
     tok[own, 0:width] = grad_ref[...]
-    lane = lax.broadcasted_iota(jnp.int32, (tokens, ext), 1)
-    lane64 = jnp.where(lane >= 64, lane - 64, lane)
+    sub = lax.broadcasted_iota(jnp.int32, (ext, tokens), 0)
+    sub64 = jnp.where(sub >= 64, sub - 64, sub)
     ids = ids_ref[...]
     combine = comb_ref[...].astype(F32)
-    hot = jnp.zeros((tokens, ext), F32)
-    weight = jnp.zeros((tokens, ext), F32)
-    for k in range(ids.shape[1]):
-        same = ids[:, k : k + 1] == lane64
-        hot = jnp.where(same, 1.0, hot)
-        weight = jnp.where(same, combine[:, k : k + 1], weight)
-    lower = (iota((tokens, tokens), 1) < iota((tokens, tokens), 0)).astype(F32).astype(BF)
-    count = jnp.dot(lower, hot.astype(BF), preferred_element_type=F32)
+    hot_t = jnp.zeros((ext, tokens), F32)
+    weight_t = jnp.zeros((ext, tokens), F32)
+    for k in range(ids.shape[0]):
+        same = ids[k : k + 1, :] == sub64
+        hot_t = jnp.where(same, 1.0, hot_t)
+        weight_t = jnp.where(same, combine[k : k + 1, :], weight_t)
+    row, col = iota((tokens, tokens), 0), iota((tokens, tokens), 1)
+    lower = jnp.where(col < row, 1.0, 0.0).astype(BF)
+    same = jnp.where(col == row, 1.0, 0.0).astype(BF)
+    count = lax.dot_general(lower, hot_t.astype(BF), NT, preferred_element_type=F32)
+    hot = lax.dot_general(same, hot_t.astype(BF), NT, preferred_element_type=F32)
+    weight = lax.dot_general(same, weight_t.astype(BF), NT, preferred_element_type=F32)
+    lane = lax.broadcasted_iota(jnp.int32, (tokens, ext), 1)
     table = jnp.where(lane < 64, jnp.where(hot > 0.5, count, -1.0), weight)
     tok[own, width:full] = table.astype(BF)
 
-    pl.semaphore_wait(barrier, len(friends))
+    with jax.named_scope("barrier"):
+        pl.semaphore_wait(barrier, len(friends))
 
     def tok_copy(r):
         return pltpu.make_async_remote_copy(
@@ -203,9 +216,10 @@
 
     for step in range(2):
         h = mbit[2] if step == 0 else 1 - mbit[2]
-        for r in range(4 * step, 4 * step + 4):
-            if r > 0:
-                tok_arrival(r).wait_recv()
+        with jax.named_scope("wait_tokens"):
+            for r in range(4 * step, 4 * step + 4):
+                if r > 0:
+                    tok_arrival(r).wait_recv()
         there = rows(h * 4 * tokens, 4 * tokens)
         tables = tok[there, width:full]
         pos = lax.dot_general(selp[...], tables, NT, preferred_element_type=F32)
@@ -238,8 +252,9 @@
         plac[h] = jnp.where(hit, 1.0, 0.0).astype(BF)
         wplac[h] = jnp.where(hit, wgt, 0.0).astype(BF)
 
-    for copy in w_copies:
-        copy.wait()
+    with jax.named_scope("wait_weights"):
+        for copy in w_copies + s_copies:
+            copy.wait()
 
     def ret_copy(j, h, p, dc):
         here = rows(j * msg + h * half, half)
@@ -270,30 +285,22 @@
     batch = 4 * msg
     elane = lax.broadcasted_iota(jnp.int32, (batch, ext), 1)
     for k in range(4):
-        saved_wait(k)
-
-        @pl.loop(0, 16)
-        def _(i):
-            pair = pl.ds(pl.multiple_of(i * 2 * slots, 8), 2 * slots)
-            for src, dst in ((sav_g, gf), (sav_u, uf)):
-                dst[pair, :] = jnp.concatenate(
-                    [src[2 * i].astype(F32), src[2 * i + 1].astype(F32)], axis=0
-                )
-
-        if k < 3:
-            saved_start(k + 1)
-        for j in range(4 * k, 4 * k + 4):
-            if j >= 2:
+        with jax.named_scope("permute_saved"):
+            permute_saved(k)
+        with jax.named_scope("wait_rows"):
+            for j in range(4 * k, 4 * k + 4):
+                if j >= 2:
+                    for h in range(2):
+                        dis_arrival(j, h).wait_recv()
+            if k == 0:
                 for h in range(2):
-                    dis_arrival(j, h).wait_recv()
-        if k == 0:
-            for h in range(2):
-                dis_arrival(1 - c, h).wait_recv()
-                dis_self(h).wait()
+                    dis_arrival(1 - c, h).wait_recv()
+                    dis_self(h).wait()
         buf = gb.at[pl.ds((k % 2) * batch, batch)]
         load = pltpu.make_async_copy(recv.at[pl.ds(k * batch, batch)], buf, l_sem.at[4])
-        load.start()
-        load.wait()
+        with jax.named_scope("load_rows"):
+            load.start()
+            load.wait()
 
         cacc[...] = jnp.zeros_like(cacc)
         tile = 256
@@ -302,7 +309,7 @@
         def _(n):
             cols = pl.ds(pl.multiple_of(n * tile, tile), tile)
             dh = lax.dot_general(buf[...], dw[cols, :], NT, preferred_element_type=F32)
-            g, u = gf[:, cols], uf[:, cols]
+            g, u = gf[:, cols].astype(F32), uf[:, cols].astype(F32)
             sg = jax.nn.sigmoid(g)
             a = g * sg
             prod = a * u * dh
@@ -313,13 +320,14 @@
             dg[:, cols] = (dh * u * sg * (1.0 + g * (1.0 - sg))).astype(BF)
             du[:, cols] = (dh * a).astype(BF)
 
-        for j in range(4 * k, 4 * k + 4):
-            if j >= 2:
+        with jax.named_scope("wait_stage"):
+            for j in range(4 * k, 4 * k + 4):
+                if j >= 2:
+                    for h in range(2):
+                        dis_copy(j, h, j // 2, j % 2).wait_send()
+            if k == 0:
                 for h in range(2):
-                    dis_copy(j, h, j // 2, j % 2).wait_send()
-        if k == 0:
-            for h in range(2):
-                dis_copy(1 - c, h, 0, 1 - c).wait_send()
+                    dis_copy(1 - c, h, 0, 1 - c).wait_send()
 
         here = pl.ds(k * batch, batch)
         comb = jnp.sum(cacc[...], axis=1, keepdims=True)
@@ -357,18 +365,20 @@
 
     for step in range(2):
         h = 1 - mbit[2] if step == 0 else mbit[2]
-        for j in range(2, 16):
-            ret_arrival(j, h).wait_recv()
-        ret_arrival(1 - c, h).wait_recv()
-        ret_self(h).wait()
+        with jax.named_scope("wait_returns"):
+            for j in range(2, 16):
+                ret_arrival(j, h).wait_recv()
+            ret_arrival(1 - c, h).wait_recv()
+            ret_self(h).wait()
         loads = (
             pltpu.make_async_copy(ret.at[h, :, pl.ds(0, width)], gb, l_sem.at[5]),
             pltpu.make_async_copy(ret.at[h, :, pl.ds(width, ext)], rc, l_sem.at[6]),
         )
-        for load in loads:
-            load.start()
-        for load in loads:
-            load.wait()
+        with jax.named_scope("load_returns"):
+            for load in loads:
+                load.start()
+            for load in loads:
+                load.wait()
         there = rows(h * 4 * tokens, 4 * tokens)
         tok[there, width:full] = jnp.dot(plac[h], rc[...], preferred_element_type=F32).astype(BF)
         tile = 512
@@ -382,8 +392,9 @@
             if r > 0:
                 part_copy(r).start()
 
-    for r in range(1, 8):
-        part_copy(r).wait_recv()
+    with jax.named_scope("wait_parts"):
+        for r in range(1, 8):
+            part_copy(r).wait_recv()
     tile = 512
 
     @pl.loop(0, width // tile)
@@ -398,19 +409,22 @@
     for r in range(1, 8):
         total = total + part[r * tokens : (r + 1) * tokens, width:full].astype(F32)
     total = jnp.where(lane < 64, total, 0.0)
-    klane = lax.broadcasted_iota(jnp.int32, ids.shape, 1)
+    same = jnp.where(iota((ext, ext), 0) == iota((ext, ext), 1), 1.0, 0.0).astype(BF)
+    total_t = lax.dot_general(same, total.astype(BF), NT, preferred_element_type=F32)
+    ksub = lax.broadcasted_iota(jnp.int32, ids.shape, 0)
     result = jnp.zeros(ids.shape, F32)
-    for k in range(ids.shape[1]):
-        value = jnp.sum(jnp.where(ids[:, k : k + 1] == lane, total, 0.0), axis=1, keepdims=True)
-        result = jnp.where(klane == k, value, result)
+    for k in range(ids.shape[0]):
+        value = jnp.sum(jnp.where(ids[k : k + 1, :] == sub, total_t, 0.0), axis=0, keepdims=True)
+        result = jnp.where(ksub == k, value, result)
     outc_ref[...] = result.astype(BF)
 
-    for r in range(1, 8):
-        part_copy(r).wait_send()
-    for h in range(2):
-        ret_copy(1 - c, h, 0, 1 - c).wait_send()
-        for j in range(2, 16):
-            ret_copy(j, h, j // 2, j % 2).wait_send()
+    with jax.named_scope("wait_sends"):
+        for r in range(1, 8):
+            part_copy(r).wait_send()
+        for h in range(2):
+            ret_copy(1 - c, h, 0, 1 - c).wait_send()
+            for j in range(2, 16):
+                ret_copy(j, h, j // 2, j % 2).wait_send()
 
 
 def body(grad_out, expert_ids, combine, gate_saved, up_saved, gate_weight, up_weight, down_weight):
@@ -428,7 +442,7 @@
         functools.partial(kernel, tokens, slots, width, hidden),
         out_shape=(
             jax.ShapeDtypeStruct((tokens, width), BF),
-            jax.ShapeDtypeStruct((tokens, top), BF),
+            jax.ShapeDtypeStruct((top, tokens), BF),
             jax.ShapeDtypeStruct((2 * cover, width), BF),
             jax.ShapeDtypeStruct((2, cover, full), BF),
         ),
@@ -440,12 +454,13 @@
             pltpu.VMEM((width, hidden), BF),
             pltpu.VMEM((width, hidden), BF),
             pltpu.VMEM((hidden, width), BF),
-            pltpu.VMEM((32, slots, hidden), BF),
-            pltpu.VMEM((32, slots, hidden), BF),
-            pltpu.VMEM((batch, hidden), F32),
-            pltpu.VMEM((batch, hidden), F32),
+            pltpu.VMEM((2 * cover, hidden), BF),
+            pltpu.VMEM((2 * cover, hidden), BF),
             pltpu.VMEM((batch, hidden), BF),
             pltpu.VMEM((batch, hidden), BF),
+            pltpu.VMEM((batch, hidden), BF),
+            pltpu.VMEM((batch, hidden), BF),
+            pltpu.VMEM((batch, 2 * cover), BF),
             pltpu.VMEM((batch, 128), F32),
             pltpu.VMEM((cover, width), BF),
             pltpu.VMEM((cover, 128), BF),
@@ -455,8 +470,7 @@
             pltpu.VMEM((2, 4 * tokens, cover), BF),
             pltpu.VMEM((2, 4 * tokens, cover), BF),
             pltpu.VMEM((8 * tokens, full), BF),
-            dma((3,)),
-            dma((2, 32)),
+            dma((5,)),
             dma((7,)),
             dma((8,)),
             dma((8,)),
@@ -475,8 +489,17 @@
             bytes_accessed=80_000_000,
             transcendentals=sources * slots * hidden,
         ),
-    )(grad_out, expert_ids, combine, gate_saved, up_saved, gate_weight, up_weight, down_weight)
-    return out[0], out[1]
+    )(
+        grad_out,
+        expert_ids.T,
+        combine.T,
+        gate_saved.transpose(1, 0, 2).reshape(2 * cover, hidden),
+        up_saved.transpose(1, 0, 2).reshape(2 * cover, hidden),
+        gate_weight,
+        up_weight,
+        down_weight,
+    )
+    return out[0], out[1].T
 
 
 def solution(mesh):

time: 272 us -> 271 us (level)
  the two profiles are of different devices: /device:TPU:0 before, /device:TPU:57 now
where the time goes in v2:
time: 271 us; the launch traced here: 270 us
  Pallas kernels  266 us (98%)
  local copies, waits for them, and re-layouts  3.23 us (1%)
    pallas_call x1, Pallas kernels, body(): pl.pallas_call(functools.partial(kernel, tokens, slots, width, hidden), o...  266 us

profile of v2, /device:TPU:57, one launch (start us, length us, event | category | flops | bytes accessed | tf_op | source)
XLA Modules:
  0.0 270.4 jit_solution(7659158372490279467)
XLA Ops:
  0.6 266.5 %shard_map.95 = (bf16[80,4096]{1,0:T(8,128)(2,1)}, bf16[8,80]{1,0:T(8,128)(2,1)}, bf16[1536,4096]{1,0:T(8,128)(2,1)}, bf16[2,768,4224]{2,1,0:T(8,128)(2,1)}) custom-call(bf16[80,4096]{1,0:T(8,128)(2,1)} %grad_ref.1, s32[8,80]{1,0:T(8,128)} %bitcast.12, bf16[8,80]{1,0:T(8,128)(2,1)} %bitcast.13, bf16[1536,768]{1,0:T(8,128)(2,1)} %bitcast.10, ...), custom_call_target="tpu_custom_call" | custom-call | flops 28991029248 | bytes 80000000 | tf_op jit(solution)/shard_map/pallas_call | solution.py:441
  267.1 2.0 copy.12
  269.1 1.3 copy.13

commit v3 on v2

--- a/solution.py
+++ b/solution.py
@@ -48,7 +48,7 @@
     tokens, slots, width, hidden,
     grad_ref, ids_ref, comb_ref, gate_hbm, up_hbm, gw_hbm, uw_hbm, dw_hbm,
     out_ref, outc_ref, recv, ret,
-    tok, stage, gw, uw, dw, sav_g, sav_u, gf, uf, dg, du, perm, cacc, gb, rc, sel, selp, selw, plac, wplac, part,
+    tok, stage, gw, uw, dw, sav_g, sav_u, gf, uf, dg, du, perm, cacc, gb, sel, selp, selw, plac, wplac, part,
     w_sem, l_sem, tok_send, tok_recv, dis_send, dis_recv, ret_send, ret_recv, part_send, part_recv,
 ):
     ext = 128
@@ -148,29 +148,40 @@
     with jax.named_scope("barrier"):
         pl.semaphore_wait(barrier, len(friends))
 
-    def tok_copy(r):
-        return pltpu.make_async_remote_copy(
-            src_ref=tok.at[own],
-            dst_ref=tok.at[own],
-            send_sem=tok_send.at[r],
-            recv_sem=tok_recv.at[r],
-            device_id=device(flipped(me, r, c, inner), c),
-            device_id_type=MESH,
-        )
-
-    def tok_arrival(r):
-        there = rows(member(r) * tokens, tokens)
-        return pltpu.make_async_remote_copy(
-            src_ref=tok.at[there],
-            dst_ref=tok.at[there],
-            send_sem=tok_send.at[r],
-            recv_sem=tok_recv.at[r],
-            device_id=device(flipped(me, r, c, inner), c),
-            device_id_type=MESH,
-        )
-
-    for r in range(1, 8):
-        tok_copy(r).start()
+    third = full // 3
+    parts = [pl.ds(a * third, third) for a in range(3)]
+    def relative(a, r):
+        return sum(((r >> i) & 1) << ((a + i) % 3) for i in range(3))
+
+    def partner(a, stage_):
+        return device(flipped(me, 1 << ((a + stage_) % 3), c, inner), c)
+
+    def tok_copy(a, r, stage_):
+        block = tok.at[rows(member(relative(a, r)) * tokens, tokens), parts[a]]
+        return pltpu.make_async_remote_copy(
+            src_ref=block,
+            dst_ref=block,
+            send_sem=tok_send.at[a * 8 + r + (1 << stage_)],
+            recv_sem=tok_recv.at[a * 8 + r + (1 << stage_)],
+            device_id=partner(a, stage_),
+            device_id_type=MESH,
+        )
+
+    def tok_arrival(a, r):
+        stage_ = r.bit_length() - 1
+        block = tok.at[rows(member(relative(a, r)) * tokens, tokens), parts[a]]
+        return pltpu.make_async_remote_copy(
+            src_ref=block,
+            dst_ref=block,
+            send_sem=tok_send.at[a * 8 + r],
+            recv_sem=tok_recv.at[a * 8 + r],
+            device_id=partner(a, stage_),
+            device_id_type=MESH,
+        )
+
+    for stage_ in range(3):
+        for a in range(3):
+            tok_copy(a, 0, stage_).start()
 
     slane = lax.broadcasted_iota(jnp.int32, (half, ext), 1)
     for i in range(16):
@@ -214,12 +225,20 @@
             device_id_type=MESH,
         )
 
+    with jax.named_scope("forward_tokens"):
+        for r in range(1, 4):
+            for a in range(3):
+                tok_arrival(a, r).wait_recv()
+                for stage_ in range(r.bit_length(), 3):
+                    tok_copy(a, r, stage_).start()
+
     for step in range(2):
         h = mbit[2] if step == 0 else 1 - mbit[2]
         with jax.named_scope("wait_tokens"):
-            for r in range(4 * step, 4 * step + 4):
-                if r > 0:
-                    tok_arrival(r).wait_recv()
+            for r in range(4, 8):
+                for a in range(3):
+                    if (relative(a, r) >> 2) == step:
+                        tok_arrival(a, r).wait_recv()
         there = rows(h * 4 * tokens, 4 * tokens)
         tables = tok[there, width:full]
         pos = lax.dot_general(selp[...], tables, NT, preferred_element_type=F32)
@@ -256,14 +275,20 @@
         for copy in w_copies + s_copies:
             copy.wait()
 
-    def ret_copy(j, h, p, dc):
+    def ret_at(j, h, a):
+        return j * 2 + h if a is None else 32 + ((j - 12) * 2 + h) * 3 + a
+
+    def ret_cols(a):
+        return pl.ds(0, full) if a is None else parts[a]
+
+    def ret_copy(j, h, p, dc, a=None):
         here = rows(j * msg + h * half, half)
         there = rows((2 * p + c) * half, half)
         return pltpu.make_async_remote_copy(
-            src_ref=stage.at[here],
-            dst_ref=ret.at[h, there],
-            send_sem=ret_send.at[j * 2 + h],
-            recv_sem=ret_recv.at[(2 * p + c) * 2 + h],
+            src_ref=stage.at[here, ret_cols(a)],
+            dst_ref=ret.at[h, there, ret_cols(a)],
+            send_sem=ret_send.at[ret_at(j, h, a)],
+            recv_sem=ret_recv.at[ret_at(2 * p + c, h, a)],
             device_id=device(flipped(me, FLIPS[p], dc, outer), dc),
             device_id_type=MESH,
         )
@@ -272,12 +297,12 @@
         here = rows(c * msg + h * half, half)
         return pltpu.make_async_copy(stage.at[here], ret.at[h, rows(c * half, half)], l_sem.at[2 + h])
 
-    def ret_arrival(j, h):
-        return pltpu.make_async_remote_copy(
-            src_ref=stage.at[rows(j * msg + h * half, half)],
-            dst_ref=ret.at[h, rows(j * half, half)],
-            send_sem=ret_send.at[j * 2 + h],
-            recv_sem=ret_recv.at[j * 2 + h],
+    def ret_arrival(j, h, a=None):
+        return pltpu.make_async_remote_copy(
+            src_ref=stage.at[rows(j * msg + h * half, half), ret_cols(a)],
+            dst_ref=ret.at[h, rows(j * half, half), ret_cols(a)],
+            send_sem=ret_send.at[ret_at(j, h, a)],
+            recv_sem=ret_recv.at[ret_at(j, h, a)],
             device_id=device(me, 1 - c),
             device_id_type=MESH,
         )
@@ -332,82 +357,116 @@
         here = pl.ds(k * batch, batch)
         comb = jnp.sum(cacc[...], axis=1, keepdims=True)
         stage[here, width:full] = jnp.where(elane == my_expert, comb, 0.0).astype(BF)
-        xtile = 512
-
-        @pl.loop(0, width // xtile)
-        def _(n):
-            cols = pl.ds(pl.multiple_of(n * xtile, xtile), xtile)
+        for a in range(3):
+            cols = pl.ds(a * third, min(third, width - a * third))
             x = lax.dot_general(dg[...], gw[cols, :], NT, preferred_element_type=F32)
             x = x + lax.dot_general(du[...], uw[cols, :], NT, preferred_element_type=F32)
             stage[here, cols] = x.astype(BF)
-
+            if k == 3:
+                for j in range(12, 16):
+                    for h in range(2):
+                        ret_copy(j, h, j // 2, j % 2, a).start()
         if k == 0:
             for h in range(2):
                 ret_self(h).start()
                 ret_copy(1 - c, h, 0, 1 - c).start()
-        for j in range(4 * k, 4 * k + 4):
-            if j >= 2:
+        if k < 3:
+            for j in range(max(4 * k, 2), 4 * k + 4):
                 for h in range(2):
                     ret_copy(j, h, j // 2, j % 2).start()
 
-    for r in range(1, 8):
-        tok_copy(r).wait_send()
-
-    def part_copy(r):
-        return pltpu.make_async_remote_copy(
-            src_ref=tok.at[rows(member(r) * tokens, tokens)],
-            dst_ref=part.at[pl.ds(r * tokens, tokens)],
-            send_sem=part_send.at[r],
-            recv_sem=part_recv.at[r],
-            device_id=device(flipped(me, r, c, inner), c),
-            device_id_type=MESH,
-        )
-
-    for step in range(2):
-        h = 1 - mbit[2] if step == 0 else mbit[2]
-        with jax.named_scope("wait_returns"):
-            for j in range(2, 16):
+    for a in range(3):
+        for r in range(1, 8):
+            tok_arrival(a, r).wait_send()
+
+    def part_copy(a, r):
+        stage_ = r.bit_length() - 1
+        return pltpu.make_async_remote_copy(
+            src_ref=tok.at[rows(member(relative(a, r)) * tokens, tokens), parts[a]],
+            dst_ref=part.at[pl.ds(r * tokens, tokens), parts[a]],
+            send_sem=part_send.at[a * 8 + r],
+            recv_sem=part_recv.at[a * 8 + r],
+            device_id=partner(a, stage_),
+            device_id_type=MESH,
+        )
+
+    def combine_part(a):
+        loads = []
+        for h in range(2):
+            loads.append(
+                pltpu.make_async_copy(
+                    ret.at[h, :, parts[a]], gb.at[:, pl.ds(h * third, third)], l_sem.at[5 + h]
+                )
+            )
+        with jax.named_scope("load_returns"):
+            for load in loads:
+                load.start()
+        for h, load in enumerate(loads):
+            load.wait()
+            there = pl.ds(h * 4 * tokens, 4 * tokens)
+            size = min(third, width - a * third)
+            got = gb[:, h * third : h * third + size]
+            tok[there, a * third : a * third + size] = jnp.dot(
+                wplac[h], got, preferred_element_type=F32
+            ).astype(BF)
+            if size < third:
+                got = gb[:, h * third + size : (h + 1) * third]
+                tok[there, width:full] = jnp.dot(plac[h], got, preferred_element_type=F32).astype(BF)
+        for r in range(4, 8):
+            part_copy(a, r).start()
+
+    def gathered(a, r, first):
+        cols = slice(a * third, (a + 1) * third)
+        total = tok[rows(member(relative(a, r)) * tokens, tokens), cols].astype(F32)
+        for stage_ in range(2, first - 1, -1):
+            at = r + (1 << stage_)
+            total = total + part[at * tokens : (at + 1) * tokens, cols].astype(F32)
+        return total
+
+    def pass_on(a, stage_):
+        with jax.named_scope("wait_parts"):
+            for r in range(1 << stage_, 2 << stage_):
+                part_copy(a, r).wait_recv()
+        if stage_ == 0:
+            return
+        for r in range(1 << (stage_ - 1), 1 << stage_):
+            cols = slice(a * third, (a + 1) * third)
+            tok[rows(member(relative(a, r)) * tokens, tokens), cols] = gathered(a, r, stage_).astype(BF)
+            part_copy(a, r).start()
+
+    with jax.named_scope("wait_returns"):
+        for h in range(2):
+            for j in range(2, 12):
                 ret_arrival(j, h).wait_recv()
             ret_arrival(1 - c, h).wait_recv()
             ret_self(h).wait()
-        loads = (
-            pltpu.make_async_copy(ret.at[h, :, pl.ds(0, width)], gb, l_sem.at[5]),
-            pltpu.make_async_copy(ret.at[h, :, pl.ds(width, ext)], rc, l_sem.at[6]),
-        )
-        with jax.named_scope("load_returns"):
-            for load in loads:
-                load.start()
-            for load in loads:
-                load.wait()
-        there = rows(h * 4 * tokens, 4 * tokens)
-        tok[there, width:full] = jnp.dot(plac[h], rc[...], preferred_element_type=F32).astype(BF)
-        tile = 512
-
-        @pl.loop(0, width // tile)
-        def _(n):
-            cols = pl.ds(pl.multiple_of(n * tile, tile), tile)
-            tok[there, cols] = jnp.dot(wplac[h], gb[:, cols], preferred_element_type=F32).astype(BF)
-
-        for r in range(4 - 4 * step, 8 - 4 * step):
-            if r > 0:
-                part_copy(r).start()
-
-    with jax.named_scope("wait_parts"):
-        for r in range(1, 8):
-            part_copy(r).wait_recv()
-    tile = 512
-
-    @pl.loop(0, width // tile)
-    def _(n):
-        cols = pl.ds(pl.multiple_of(n * tile, tile), tile)
-        total = tok[own, cols].astype(F32)
-        for r in range(1, 8):
-            total = total + part[r * tokens : (r + 1) * tokens, cols].astype(F32)
-        out_ref[:, cols] = total.astype(BF)
-
-    total = tok[own, width:full].astype(F32)
-    for r in range(1, 8):
-        total = total + part[r * tokens : (r + 1) * tokens, width:full].astype(F32)
+
+    def wait_last(a):
+        with jax.named_scope("wait_last"):
+            for h in range(2):
+                for j in range(12, 16):
+                    ret_arrival(j, h, a).wait_recv()
+
+    wait_last(0)
+    combine_part(0)
+    wait_last(1)
+    combine_part(1)
+    pass_on(0, 2)
+    wait_last(2)
+    combine_part(2)
+    pass_on(1, 2)
+    pass_on(0, 1)
+    pass_on(2, 2)
+    pass_on(1, 1)
+    pass_on(2, 1)
+    for a in range(3):
+        pass_on(a, 0)
+        total = gathered(a, 0, 0)
+        if a < 2:
+            out_ref[:, a * third : (a + 1) * third] = total.astype(BF)
+        else:
+            out_ref[:, 2 * third : width] = total[:, : width - 2 * third].astype(BF)
+            total = total[:, width - 2 * third :]
     total = jnp.where(lane < 64, total, 0.0)
     same = jnp.where(iota((ext, ext), 0) == iota((ext, ext), 1), 1.0, 0.0).astype(BF)
     total_t = lax.dot_general(same, total.astype(BF), NT, preferred_element_type=F32)
@@ -419,12 +478,16 @@
     outc_ref[...] = result.astype(BF)
 
     with jax.named_scope("wait_sends"):
-        for r in range(1, 8):
-            part_copy(r).wait_send()
+        for a in range(3):
+            for r in range(1, 8):
+                part_copy(a, r).wait_send()
         for h in range(2):
             ret_copy(1 - c, h, 0, 1 - c).wait_send()
-            for j in range(2, 16):
+            for j in range(2, 12):
                 ret_copy(j, h, j // 2, j % 2).wait_send()
+            for j in range(12, 16):
+                for a in range(3):
+                    ret_copy(j, h, j // 2, j % 2, a).wait_send()
 
 
 def body(grad_out, expert_ids, combine, gate_saved, up_saved, gate_weight, up_weight, down_weight):
@@ -463,7 +526,6 @@
             pltpu.VMEM((batch, 2 * cover), BF),
             pltpu.VMEM((batch, 128), F32),
             pltpu.VMEM((cover, width), BF),
-            pltpu.VMEM((cover, 128), BF),
             pltpu.VMEM((cover, 4 * tokens), BF),
             pltpu.VMEM((cover, 128), BF),
             pltpu.VMEM((cover, 128), BF),
@@ -472,14 +534,14 @@
             pltpu.VMEM((8 * tokens, full), BF),
             dma((5,)),
             dma((7,)),
-            dma((8,)),
-            dma((8,)),
+            dma((24,)),
+            dma((24,)),
             dma((32,)),
             dma((32,)),
-            dma((32,)),
-            dma((32,)),
-            dma((8,)),
-            dma((8,)),
+            dma((56,)),
+            dma((56,)),
+            dma((24,)),
+            dma((24,)),
         ],
         compiler_params=pltpu.CompilerParams(
             collective_id=0, has_side_effects=True, vmem_limit_bytes=66 * 1000 * 1000

time: 271 us -> 234 us (0.86)
  the two profiles are of different devices: /device:TPU:57 before, /device:TPU:0 now
where the time goes in v3:
time: 234 us
  Pallas kernels  230 us (98%)
  local copies, waits for them, and re-layouts  3.23 us (1%)
    pallas_call x1, Pallas kernels, body(): pl.pallas_call(functools.partial(kernel, tokens, slots, width, hidden), o...  230 us

profile of v3, /device:TPU:0, one launch (start us, length us, event | category | flops | bytes accessed | tf_op | source)
XLA Modules:
  0.0 233.5 jit_solution(1760285149090173054)
XLA Ops:
  0.6 229.7 %shard_map.95 = (bf16[80,4096]{1,0:T(8,128)(2,1)}, bf16[8,80]{1,0:T(8,128)(2,1)}, bf16[1536,4096]{1,0:T(8,128)(2,1)}, bf16[2,768,4224]{2,1,0:T(8,128)(2,1)}) custom-call(bf16[80,4096]{1,0:T(8,128)(2,1)} %grad_ref.1, s32[8,80]{1,0:T(8,128)} %bitcast.12, bf16[8,80]{1,0:T(8,128)(2,1)} %bitcast.13, bf16[1536,768]{1,0:T(8,128)(2,1)} %bitcast.10, ...), custom_call_target="tpu_custom_call" | custom-call | flops 28991029248 | bytes 80000000 | tf_op jit(solution)/shard_map/pallas_call | solution.py:504
  230.3 2.0 copy.12
  232.3 1.3 copy.13

commit v4 on v3

--- a/solution.py
+++ b/solution.py
@@ -150,6 +150,9 @@
 
     third = full // 3
     parts = [pl.ds(a * third, third) for a in range(3)]
+    piece = 6 * ext
+    sums = [pl.ds(a * piece, min(piece, full - a * piece)) for a in range(-(-full // piece))]
+
     def relative(a, r):
         return sum(((r >> i) & 1) << ((a + i) % 3) for i in range(3))
 
@@ -225,6 +228,34 @@
             device_id_type=MESH,
         )
 
+    def dis_start(h, k):
+        if k == 0:
+            dis_self(h).start()
+            dis_copy(1 - c, h, 0, 1 - c).start()
+        for j in range(max(4 * k, 2), 4 * k + 4):
+            dis_copy(j, h, j // 2, j % 2).start()
+
+    def dis_sent(k):
+        if k == 0:
+            for h in range(2):
+                dis_copy(1 - c, h, 0, 1 - c).wait_send()
+        for j in range(max(4 * k, 2), 4 * k + 4):
+            for h in range(2):
+                dis_copy(j, h, j // 2, j % 2).wait_send()
+
+    def select(step, h, later):
+        there = rows(h * 4 * tokens, 4 * tokens)
+        size = cover // 2
+        tile = 512
+
+        @pl.loop(0, width // tile)
+        def _(n):
+            cols = pl.ds(pl.multiple_of(n * tile, tile), tile)
+            chosen = sel[step, later * size : (later + 1) * size]
+            got = jnp.dot(chosen, tok[there, cols], preferred_element_type=F32).astype(BF)
+            for i in range(8):
+                stage[rows((8 * later + i) * msg + h * half, half), cols] = got[i * half : (i + 1) * half]
+
     with jax.named_scope("forward_tokens"):
         for r in range(1, 4):
             for a in range(3):
@@ -244,22 +275,14 @@
         pos = lax.dot_general(selp[...], tables, NT, preferred_element_type=F32)
         slot, four = slot_of(iota((cover, 1), 0))
         owner = owner_of(iota((1, 4 * tokens), 1))
-        sel[...] = jnp.where((pos == slot) & (four == owner), 1.0, 0.0).astype(BF)
-
-        tile = 512
-
-        @pl.loop(0, width // tile)
-        def _(n):
-            cols = pl.ds(pl.multiple_of(n * tile, tile), tile)
-            got = jnp.dot(sel[...], tok[there, cols], preferred_element_type=F32).astype(BF)
-            for i in range(16):
-                stage[rows(i * msg + h * half, half), cols] = got[i * half : (i + 1) * half]
-
-        dis_self(h).start()
-        dis_copy(1 - c, h, 0, 1 - c).start()
-        for p in range(1, 8):
-            for dc in range(2):
-                dis_copy(2 * p + dc, h, p, dc).start()
+        sel[step] = jnp.where((pos == slot) & (four == owner), 1.0, 0.0).astype(BF)
+
+        select(step, h, 0)
+        dis_start(h, 0)
+        dis_start(h, 1)
+
+    for step in range(2):
+        select(step, mbit[2] if step == 0 else 1 - mbit[2], 1)
 
     slot, four = slot_of(iota((1, cover), 1))
     owner = owner_of(iota((4 * tokens, 1), 0))
@@ -276,10 +299,10 @@
             copy.wait()
 
     def ret_at(j, h, a):
-        return j * 2 + h if a is None else 32 + ((j - 12) * 2 + h) * 3 + a
+        return j * 2 + h if a is None else 32 + ((j - 12) * 2 + h) * len(sums) + a
 
     def ret_cols(a):
-        return pl.ds(0, full) if a is None else parts[a]
+        return pl.ds(0, full) if a is None else sums[a]
 
     def ret_copy(j, h, p, dc, a=None):
         here = rows(j * msg + h * half, half)
@@ -306,6 +329,11 @@
             device_id=device(me, 1 - c),
             device_id_type=MESH,
         )
+
+    with jax.named_scope("wait_first"):
+        dis_sent(0)
+        for h in range(2):
+            dis_start(h, 2)
 
     batch = 4 * msg
     elane = lax.broadcasted_iota(jnp.int32, (batch, ext), 1)
@@ -346,19 +374,18 @@
             du[:, cols] = (dh * a).astype(BF)
 
         with jax.named_scope("wait_stage"):
-            for j in range(4 * k, 4 * k + 4):
-                if j >= 2:
-                    for h in range(2):
-                        dis_copy(j, h, j // 2, j % 2).wait_send()
             if k == 0:
+                dis_sent(1)
                 for h in range(2):
-                    dis_copy(1 - c, h, 0, 1 - c).wait_send()
+                    dis_start(h, 3)
+            elif k > 1:
+                dis_sent(k)
 
         here = pl.ds(k * batch, batch)
         comb = jnp.sum(cacc[...], axis=1, keepdims=True)
         stage[here, width:full] = jnp.where(elane == my_expert, comb, 0.0).astype(BF)
-        for a in range(3):
-            cols = pl.ds(a * third, min(third, width - a * third))
+        for a in range(len(sums)):
+            cols = pl.ds(a * piece, min(piece, width - a * piece))
             x = lax.dot_general(dg[...], gw[cols, :], NT, preferred_element_type=F32)
             x = x + lax.dot_general(du[...], uw[cols, :], NT, preferred_element_type=F32)
             stage[here, cols] = x.astype(BF)
@@ -382,8 +409,8 @@
     def part_copy(a, r):
         stage_ = r.bit_length() - 1
         return pltpu.make_async_remote_copy(
-            src_ref=tok.at[rows(member(relative(a, r)) * tokens, tokens), parts[a]],
-            dst_ref=part.at[pl.ds(r * tokens, tokens), parts[a]],
+            src_ref=tok.at[rows(member(relative(a, r)) * tokens, tokens), sums[a]],
+            dst_ref=part.at[pl.ds(r * tokens, tokens), sums[a]],
             send_sem=part_send.at[a * 8 + r],
             recv_sem=part_recv.at[a * 8 + r],
             device_id=partner(a, stage_),
@@ -395,7 +422,7 @@
         for h in range(2):
             loads.append(
                 pltpu.make_async_copy(
-                    ret.at[h, :, parts[a]], gb.at[:, pl.ds(h * third, third)], l_sem.at[5 + h]
+                    ret.at[h, :, sums[a]], gb.at[:, pl.ds(h * piece, sums[a].size)], l_sem.at[5 + h]
                 )
             )
         with jax.named_scope("load_returns"):
@@ -404,19 +431,19 @@
         for h, load in enumerate(loads):
             load.wait()
             there = pl.ds(h * 4 * tokens, 4 * tokens)
-            size = min(third, width - a * third)
-            got = gb[:, h * third : h * third + size]
-            tok[there, a * third : a * third + size] = jnp.dot(
+            size = min(piece, width - a * piece)
+            got = gb[:, h * piece : h * piece + size]
+            tok[there, a * piece : a * piece + size] = jnp.dot(
                 wplac[h], got, preferred_element_type=F32
             ).astype(BF)
-            if size < third:
-                got = gb[:, h * third + size : (h + 1) * third]
+            if size < sums[a].size:
+                got = gb[:, h * piece + size : h * piece + size + ext]
                 tok[there, width:full] = jnp.dot(plac[h], got, preferred_element_type=F32).astype(BF)
         for r in range(4, 8):
             part_copy(a, r).start()
 
     def gathered(a, r, first):
-        cols = slice(a * third, (a + 1) * third)
+        cols = sums[a]
         total = tok[rows(member(relative(a, r)) * tokens, tokens), cols].astype(F32)
         for stage_ in range(2, first - 1, -1):
             at = r + (1 << stage_)
@@ -430,7 +457,7 @@
         if stage_ == 0:
             return
         for r in range(1 << (stage_ - 1), 1 << stage_):
-            cols = slice(a * third, (a + 1) * third)
+            cols = sums[a]
             tok[rows(member(relative(a, r)) * tokens, tokens), cols] = gathered(a, r, stage_).astype(BF)
             part_copy(a, r).start()
 
@@ -447,26 +474,25 @@
                 for j in range(12, 16):
                     ret_arrival(j, h, a).wait_recv()
 
-    wait_last(0)
-    combine_part(0)
-    wait_last(1)
-    combine_part(1)
-    pass_on(0, 2)
-    wait_last(2)
-    combine_part(2)
-    pass_on(1, 2)
-    pass_on(0, 1)
-    pass_on(2, 2)
-    pass_on(1, 1)
-    pass_on(2, 1)
-    for a in range(3):
+    def finish(a):
         pass_on(a, 0)
         total = gathered(a, 0, 0)
-        if a < 2:
-            out_ref[:, a * third : (a + 1) * third] = total.astype(BF)
-        else:
-            out_ref[:, 2 * third : width] = total[:, : width - 2 * third].astype(BF)
-            total = total[:, width - 2 * third :]
+        size = min(piece, width - a * piece)
+        out_ref[:, a * piece : a * piece + size] = total[:, :size].astype(BF)
+        return total
+
+    count = len(sums)
+    for a in range(count + 3):
+        if a < count:
+            wait_last(a)
+            combine_part(a)
+        if 1 <= a < count + 1:
+            pass_on(a - 1, 2)
+        if 2 <= a < count + 2:
+            pass_on(a - 2, 1)
+        if a >= 3:
+            total = finish(a - 3)
+    total = total[:, width % piece :]
     total = jnp.where(lane < 64, total, 0.0)
     same = jnp.where(iota((ext, ext), 0) == iota((ext, ext), 1), 1.0, 0.0).astype(BF)
     total_t = lax.dot_general(same, total.astype(BF), NT, preferred_element_type=F32)
@@ -478,7 +504,7 @@
     outc_ref[...] = result.astype(BF)
 
     with jax.named_scope("wait_sends"):
-        for a in range(3):
+        for a in range(count):
             for r in range(1, 8):
                 part_copy(a, r).wait_send()
         for h in range(2):
@@ -486,7 +512,7 @@
             for j in range(2, 12):
                 ret_copy(j, h, j // 2, j % 2).wait_send()
             for j in range(12, 16):
-                for a in range(3):
+                for a in range(count):
                     ret_copy(j, h, j // 2, j % 2, a).wait_send()
 
 
@@ -526,7 +552,7 @@
             pltpu.VMEM((batch, 2 * cover), BF),
             pltpu.VMEM((batch, 128), F32),
             pltpu.VMEM((cover, width), BF),
-            pltpu.VMEM((cover, 4 * tokens), BF),
+            pltpu.VMEM((2, cover, 4 * tokens), BF),
             pltpu.VMEM((cover, 128), BF),
             pltpu.VMEM((cover, 128), BF),
             pltpu.VMEM((2, 4 * tokens, cover), BF),
@@ -538,10 +564,10 @@
             dma((24,)),
             dma((32,)),
             dma((32,)),
-            dma((56,)),
-            dma((56,)),
-            dma((24,)),
-            dma((24,)),
+            dma((32 + 48,)),
+            dma((32 + 48,)),
+            dma((48,)),
+            dma((48,)),
         ],
         compiler_params=pltpu.CompilerParams(
             collective_id=0, has_side_effects=True, vmem_limit_bytes=66 * 1000 * 1000

time: 234 us -> 224 us (0.957); the launches traced: 234 us -> 221 us
  Pallas kernels: 230 us -> 217 us
    pallas_call x1, Pallas kernels: 230 us -> 217 us  [body(): pl.pallas_call(functools.partial(kernel, tokens, slots, width, hidden), o...]
where the time goes in v4:
time: 224 us; the launch traced here: 221 us
  Pallas kernels  217 us (97%)
  local copies, waits for them, and re-layouts  3.23 us (1%)
    pallas_call x1, Pallas kernels, body(): pl.pallas_call(functools.partial(kernel, tokens, slots, width, hidden), o...  217 us

profile of v4, /device:TPU:0, one launch (start us, length us, event | category | flops | bytes accessed | tf_op | source)
XLA Modules:
  0.0 220.9 jit_solution(7710635808695815736)
XLA Ops:
  0.6 217.1 %shard_map.95 = (bf16[80,4096]{1,0:T(8,128)(2,1)}, bf16[8,80]{1,0:T(8,128)(2,1)}, bf16[1536,4096]{1,0:T(8,128)(2,1)}, bf16[2,768,4224]{2,1,0:T(8,128)(2,1)}) custom-call(bf16[80,4096]{1,0:T(8,128)(2,1)} %grad_ref.1, s32[8,80]{1,0:T(8,128)} %bitcast.12, bf16[8,80]{1,0:T(8,128)(2,1)} %bitcast.13, bf16[1536,768]{1,0:T(8,128)(2,1)} %bitcast.10, ...), custom_call_target="tpu_custom_call" | custom-call | flops 28991029248 | bytes 80000000 | tf_op jit(solution)/shard_map/pallas_call | solution.py:530
  217.7 2.0 copy.12
  219.7 1.3 copy.13

commit v5 on v4

--- a/solution.py
+++ b/solution.py
@@ -228,12 +228,15 @@
             device_id_type=MESH,
         )
 
+    def messages(k):
+        return [(p, dc) for dc in (c, 1 - c) for p in (2 * k, 2 * k + 1) if p > 0]
+
     def dis_start(h, k):
         if k == 0:
             dis_self(h).start()
             dis_copy(1 - c, h, 0, 1 - c).start()
-        for j in range(max(4 * k, 2), 4 * k + 4):
-            dis_copy(j, h, j // 2, j % 2).start()
+        for p, dc in messages(k):
+            dis_copy(2 * p + dc, h, p, dc).start()
 
     def dis_sent(k):
         if k == 0:
@@ -282,7 +285,9 @@
         dis_start(h, 1)
 
     for step in range(2):
-        select(step, mbit[2] if step == 0 else 1 - mbit[2], 1)
+        h = mbit[2] if step == 0 else 1 - mbit[2]
+        select(step, h, 1)
+        dis_start(h, 2)
 
     slot, four = slot_of(iota((1, cover), 1))
     owner = owner_of(iota((4 * tokens, 1), 0))
@@ -299,7 +304,7 @@
             copy.wait()
 
     def ret_at(j, h, a):
-        return j * 2 + h if a is None else 32 + ((j - 12) * 2 + h) * len(sums) + a
+        return j * 2 + h if a is None else 32 + ((j - 8) * 2 + h) * len(sums) + a
 
     def ret_cols(a):
         return pl.ds(0, full) if a is None else sums[a]
@@ -333,7 +338,12 @@
     with jax.named_scope("wait_first"):
         dis_sent(0)
         for h in range(2):
-            dis_start(h, 2)
+            dis_start(h, 3)
+
+    def ret_part(k, a):
+        for p, dc in messages(k):
+            for h in range(2):
+                ret_copy(2 * p + dc, h, p, dc, a).start()
 
     batch = 4 * msg
     elane = lax.broadcasted_iota(jnp.int32, (batch, ext), 1)
@@ -374,11 +384,7 @@
             du[:, cols] = (dh * a).astype(BF)
 
         with jax.named_scope("wait_stage"):
-            if k == 0:
-                dis_sent(1)
-                for h in range(2):
-                    dis_start(h, 3)
-            elif k > 1:
+            if k > 0:
                 dis_sent(k)
 
         here = pl.ds(k * batch, batch)
@@ -389,18 +395,20 @@
             x = lax.dot_general(dg[...], gw[cols, :], NT, preferred_element_type=F32)
             x = x + lax.dot_general(du[...], uw[cols, :], NT, preferred_element_type=F32)
             stage[here, cols] = x.astype(BF)
-            if k == 3:
-                for j in range(12, 16):
-                    for h in range(2):
-                        ret_copy(j, h, j // 2, j % 2, a).start()
+            if k >= 2 and a < len(sums) // 2:
+                ret_part(k, a)
+        if k == 3:
+            for a in range(len(sums) // 2, len(sums)):
+                for b in (2, 3):
+                    ret_part(b, a)
         if k == 0:
             for h in range(2):
                 ret_self(h).start()
                 ret_copy(1 - c, h, 0, 1 - c).start()
-        if k < 3:
-            for j in range(max(4 * k, 2), 4 * k + 4):
+        if k < 2:
+            for p, dc in messages(k):
                 for h in range(2):
-                    ret_copy(j, h, j // 2, j % 2).start()
+                    ret_copy(2 * p + dc, h, p, dc).start()
 
     for a in range(3):
         for r in range(1, 8):
@@ -463,7 +471,7 @@
 
     with jax.named_scope("wait_returns"):
         for h in range(2):
-            for j in range(2, 12):
+            for j in range(2, 8):
                 ret_arrival(j, h).wait_recv()
             ret_arrival(1 - c, h).wait_recv()
             ret_self(h).wait()
@@ -471,7 +479,7 @@
     def wait_last(a):
         with jax.named_scope("wait_last"):
             for h in range(2):
-                for j in range(12, 16):
+                for j in range(8, 16):
                     ret_arrival(j, h, a).wait_recv()
 
     def finish(a):
@@ -509,9 +517,9 @@
                 part_copy(a, r).wait_send()
         for h in range(2):
             ret_copy(1 - c, h, 0, 1 - c).wait_send()
-            for j in range(2, 12):
+            for j in range(2, 8):
                 ret_copy(j, h, j // 2, j % 2).wait_send()
-            for j in range(12, 16):
+            for j in range(8, 16):
                 for a in range(count):
                     ret_copy(j, h, j // 2, j % 2, a).wait_send()
 
@@ -564,8 +572,8 @@
             dma((24,)),
             dma((32,)),
             dma((32,)),
-            dma((32 + 48,)),
-            dma((32 + 48,)),
+            dma((32 + 96,)),
+            dma((32 + 96,)),
             dma((48,)),
             dma((48,)),
         ],

time: 224 us -> 231 us (1.031)
  Pallas kernels: 217 us -> 222 us
    pallas_call x1, Pallas kernels: 217 us -> 222 us  [body(): pl.pallas_call(functools.partial(kernel, tokens, slots, width, hidden), o...]
where the time goes in v5:
time: 231 us; the launch traced here: 226 us
  Pallas kernels  222 us (96%)
  local copies, waits for them, and re-layouts  3.23 us (1%)
    pallas_call x1, Pallas kernels, body(): pl.pallas_call(functools.partial(kernel, tokens, slots, width, hidden), o...  222 us

profile of v5, /device:TPU:0, one launch (start us, length us, event | category | flops | bytes accessed | tf_op | source)
XLA Modules:
  0.0 226.0 jit_solution(15924490123095012552)
XLA Ops:
  0.6 222.0 %shard_map.95 = (bf16[80,4096]{1,0:T(8,128)(2,1)}, bf16[8,80]{1,0:T(8,128)(2,1)}, bf16[1536,4096]{1,0:T(8,128)(2,1)}, bf16[2,768,4224]{2,1,0:T(8,128)(2,1)}) custom-call(bf16[80,4096]{1,0:T(8,128)(2,1)} %grad_ref.1, s32[8,80]{1,0:T(8,128)} %bitcast.12, bf16[8,80]{1,0:T(8,128)(2,1)} %bitcast.13, bf16[1536,768]{1,0:T(8,128)(2,1)} %bitcast.10, ...), custom_call_target="tpu_custom_call" | custom-call | flops 28991029248 | bytes 80000000 | tf_op jit(solution)/shard_map/pallas_call | solution.py:538
  222.6 2.0 copy.12
  224.6 1.3 copy.13
